TPU v7x, 256 devices: a whole 4x4x8 slice. The times are simulated.
256 devices in a mesh: blk: 64 (over x_hi, y, z), col: 4 (over x_lo, core).
Axes of the slice: x: 4 (x_hi: 2, x_lo: 2; x = x_hi * 2 + x_lo), y: 4, z: 8, core: 2. Of those that a mesh axis runs over, the one named last changes fastest.
Arguments:
- amplitudes: bfloat16 [12288, 8192], P('blk', 'col'), may hold values from -6 to 6
- integrals: bfloat16 [65536, 8192], P('blk', 'col'), may hold values from -0.0625 to 0.0625
- allowed: int32 [8, 8, 8], replicated, may hold values 0 or 1
- partner: int32 [8, 1536], replicated, may hold values from 0 to 1535, as said below
Outputs:
- residual: bfloat16 [1536, 65536], P('col', 'blk')
Inputs may be any that keep to these rules, and one draw needn't show every extreme that they name: partner[s, partner[s, p]] = p and partner[s, p] != p for every s and p.
All inputs are finite; a program needn't handle non-finite values.
Results may differ from a plain program's by a relative error of at most 0.001.
Values may be sent and summed in bfloat16 or wider, within the bound.
A program may use at most 128 MiB of HBM per device.

v0:
```python
import jax
import jax.numpy as jnp
from jax import lax
from jax.sharding import PartitionSpec as P

NB = 8


def swapped(value, axis, distance):
    return lax.ppermute(value, axis, [(i, i ^ 1 << distance) for i in range(lax.axis_size(axis))])


def body(amplitudes, integrals, allowed, partner):
    rows_piece = amplitudes.shape[0]
    ab_rows, quarter = integrals.shape
    per_quarter = quarter // ab_rows
    position = lax.axis_index("blk")
    sector = position // NB
    member = position % NB
    column = lax.axis_index("col")
    sector_grid = lax.dynamic_index_in_dim(allowed, sector, 0, keepdims=False)
    row_flags = lax.dynamic_index_in_dim(sector_grid, member, 0, keepdims=False)
    tile_flags = lax.dynamic_slice_in_dim(row_flags, column * per_quarter, per_quarter, 0)
    contract = (((1,), (1,)), ((), ()))
    scaled = (
        integrals.reshape(ab_rows, per_quarter, ab_rows)
        * tile_flags.astype(jnp.bfloat16)[None, :, None]
    )
    weights = scaled.reshape(ab_rows, quarter)

    def apply_tiles(arrived):
        return lax.dot_general(arrived, weights, contract, preferred_element_type=jnp.float32)

    def place_rows(ladder, arrived, source):
        return lax.dynamic_update_slice_in_dim(ladder, apply_tiles(arrived), source * rows_piece, 0)

    ladder = jnp.zeros((rows_piece * NB, ab_rows), jnp.float32)
    ladder = place_rows(ladder, amplitudes, member)
    collected = amplitudes
    levels = NB.bit_length() - 1
    for bit_level in range(levels):
        incoming = swapped(collected, "blk", bit_level)
        source = (member >> bit_level ^ 1) << bit_level
        ladder = place_rows(ladder, incoming, source)
        if bit_level + 1 < levels:
            lower_half = member >> bit_level & 1 == 0
            collected = jnp.where(
                lower_half,
                jnp.concatenate([collected, incoming], axis=0),
                jnp.concatenate([incoming, collected], axis=0),
            )
    pairs_row = lax.dynamic_index_in_dim(partner, sector, 0, keepdims=False)
    summed = lax.psum_scatter(ladder, "col", scatter_dimension=0, tiled=True)
    gathered = lax.all_gather(summed, "col", axis=0, tiled=True)
    my_partners = lax.dynamic_slice_in_dim(pairs_row, column * summed.shape[0], summed.shape[0], 0)
    summed = 0.5 * (summed - jnp.take(gathered, my_partners, axis=0))
    return summed.astype(jnp.bfloat16)


def solution(mesh):
    return jax.shard_map(
        body,
        mesh=mesh,
        in_specs=(P("blk", "col"), P("blk", "col"), P(), P()),
        out_specs=P("col", "blk"),
        check_vma=False,
    )
```

profile of v0, /device:TPU:1, one launch (start us, length us, event | category | flops | bytes accessed | tf_op | source)
XLA Modules:
  0.0 400.5 jit_solution(14016882964368061248)
XLA Ops:
  6.5 0.0 reduce-scatter.2.cloned.1.call-start
  6.5 2.5 collective-permute-start
  9.0 16.5 %collective-permute-done = bf16[192,2048]{1,0:T(8,128)(2,1)S(1)} collective-permute-done((bf16[192,2048]{1,0:T(8,128)(2,1)}, bf16[192,2048]{1,0:T(8,128)(2,1)S(1)}, u32[]{:S(2)}, u32[]{:S(2)}) %collective-permute-start) | collective-permute-done | bytes 786464 | tf_op jit(solution)/shard_map/ppermute | solution.py:10
  25.5 0.0 copy-start.2
  25.5 0.9 copy-done.2
  26.4 2.0 maximum_select_fusion.1
  28.4 3.9 collective-permute-start.1
  32.3 67.5 %collective-permute-done.1 = bf16[384,2048]{1,0:T(8,128)(2,1)S(1)} collective-permute-done((bf16[384,2048]{1,0:T(8,128)(2,1)S(1)}, bf16[384,2048]{1,0:T(8,128)(2,1)S(1)}, u32[]{:S(2)}, u32[]{:S(2)}) %collective-permute-start.1) | collective-permute-done | bytes 1572896 | tf_op jit(solution)/shard_map/ppermute | solution.py:10
  99.8 2.9 maximum_select_fusion
  102.8 6.4 %collective-permute-start.2 = (bf16[768,2048]{1,0:T(8,128)(2,1)}, bf16[768,2048]{1,0:T(8,128)(2,1)}, u32[]{:S(2)}, u32[]{:S(2)}) collective-permute-start(bf16[768,2048]{1,0:T(8,128)(2,1)} %maximum_select_fusion), channel_id=1, source_target_pairs={{0,16},{4,20},{8,24},{12,28},{16,0},{20,4},{24,8},{28,12},{32,48},... | collective-permute-start | bytes 9437192 | tf_op jit(solution)/shard_map/ppermute | solution.py:10
  109.2 0.8 convert_bitcast_fusion
  110.0 0.1 broadcast_bitcast_fusion
  110.0 0.0 copy-start.1
  110.1 0.0 copy-start.4
  110.1 3.7 broadcast_in_dim.14
  113.8 0.0 copy-done.1
  113.8 0.4 copy-done.4
  114.2 0.0 copy-start.3
  114.2 2.4 fusion.21
  116.6 0.0 copy-done.3
  116.6 2.4 fusion.27
  119.0 3.1 fusion.15
  122.1 122.9 %collective-permute-done.2 = bf16[768,2048]{1,0:T(8,128)(2,1)} collective-permute-done((bf16[768,2048]{1,0:T(8,128)(2,1)}, bf16[768,2048]{1,0:T(8,128)(2,1)}, u32[]{:S(2)}, u32[]{:S(2)}) %collective-permute-start.2) | collective-permute-done | bytes 3145760 | tf_op jit(solution)/shard_map/ppermute | solution.py:10
  245.0 7.1 %fusion.8 = f32[1536,1024]{1,0:T(8,128)} fusion(f32[1536,1024]{1,0:T(8,128)} %fusion.15, s32[]{:T(128)S(6)} %select_n.98, bf16[768,2048]{1,0:T(8,128)(2,1)} %collective-permute-done.2, bf16[1024,2048]{1,0:T(8,128)(2,1)S(1)} %copy-done.4, bf16[2048]{0:T(1024)(128)(2,1)S(1)} %bitcast.24), kind=kOutput, calls=%fused_computation.10 | convolution fusion | flops 3223322624 | bytes 10489860 | tf_op jit(solution)/shard_map/dot_general | solution.py:32
  252.1 0.0 reduce-scatter.2.cloned.1.call-update
  252.2 0.0 all-gather.2.cloned.1.call-start
  252.2 65.3 %reduce-scatter.2.cloned.1.call-done = f32[384,1024]{1,0:T(8,128)} async-done(((f32[1536,1024]{1,0:T(8,128)}), f32[384,1024]{1,0:T(8,128)}) %reduce-scatter.2.cloned.1.call-update) | async-done | bytes 1572880 | tf_op jit(solution)/shard_map/reduce_scatter | solution.py:53
  317.5 0.0 all-gather.2.cloned.1.call-update
  317.5 0.8 dynamic-slice_reduce_fusion
  318.3 0.8 fusion.30
  319.2 0.0 copy-start
  319.2 67.8 %all-gather.2.cloned.1.call-done = f32[1536,1024]{1,0:T(8,128)} async-done(((f32[384,1024]{1,0:T(8,128)}), f32[1536,1024]{1,0:T(8,128)}) %all-gather.2.cloned.1.call-update) | async-done | bytes 6291472 | tf_op jit(solution)/shard_map/all_gather | solution.py:54
  387.0 5.6 %gather_fusion = f32[384,1024]{1,0:T(8,128)S(1)} fusion(f32[1536,1024]{1,0:T(8,128)} %all-gather.2.cloned.1.call-done, s32[1024]{0:T(1024)S(1)} %pad_clamp_fusion), kind=kCustom, calls=%fused_computation | custom fusion | bytes 3147264 | tf_op jit(solution)/shard_map/jit(_take)/gather | solution.py:56
  392.5 0.0 copy-done
  392.6 1.1 multiply_convert_fusion
  (3 shorter events, 0.0 us)
Async XLA Ops:
  6.5 310.9 %reduce-scatter.2.cloned.1.call-start = ((), (), s32[]{:S(2)}) async-start(), calls=%async_computation.1 | async-start | bytes 7864320 | tf_op jit(solution)/shard_map/reduce_scatter | solution.py:53
  6.5 19.0 %collective-permute-start = (bf16[192,2048]{1,0:T(8,128)(2,1)}, bf16[192,2048]{1,0:T(8,128)(2,1)S(1)}, u32[]{:S(2)}, u32[]{:S(2)}) collective-permute-start(bf16[192,2048]{1,0:T(8,128)(2,1)} %param.4), channel_id=1, source_target_pairs={{0,4},{4,0},{8,12},{12,8},{16,20},{20,16},{24,28},{28,24},{32,36},... | collective-permute-start | bytes 2359304 | tf_op jit(solution)/shard_map/ppermute | solution.py:10
  25.5 0.9 copy-start.2
  28.4 71.4 %collective-permute-start.1 = (bf16[384,2048]{1,0:T(8,128)(2,1)S(1)}, bf16[384,2048]{1,0:T(8,128)(2,1)S(1)}, u32[]{:S(2)}, u32[]{:S(2)}) collective-permute-start(bf16[384,2048]{1,0:T(8,128)(2,1)S(1)} %maximum_select_fusion.1), channel_id=1, source_target_pairs={{0,8},{4,12},{8,0},{12,4},{16,24},{20,28},{24,16},{28,20},{32,40},... | collective-permute-start | bytes 4718600 | tf_op jit(solution)/shard_map/ppermute | solution.py:10
  102.8 142.3 %collective-permute-start.2 = (bf16[768,2048]{1,0:T(8,128)(2,1)}, bf16[768,2048]{1,0:T(8,128)(2,1)}, u32[]{:S(2)}, u32[]{:S(2)}) collective-permute-start(bf16[768,2048]{1,0:T(8,128)(2,1)} %maximum_select_fusion), channel_id=1, source_target_pairs={{0,16},{4,20},{8,24},{12,28},{16,0},{20,4},{24,8},{28,12},{32,48},... | collective-permute-start | bytes 9437192 | tf_op jit(solution)/shard_map/ppermute | solution.py:10
  110.0 3.7 copy-start.1
  110.1 4.1 %copy-start.4 = (bf16[1024,2048]{1,0:T(8,128)(2,1)S(1)}, bf16[1024,2048]{1,0:T(8,128)(2,1)}, u32[]{:S(2)}) copy-start(bf16[1024,2048]{1,0:T(8,128)(2,1)} %param.5) | copy-start | bytes 12582916
  114.2 2.4 copy-start.3
  252.2 134.8 %all-gather.2.cloned.1.call-start = ((), (), s32[]{:S(2)}) async-start(), calls=%async_computation.2 | async-start | bytes 7864320 | tf_op jit(solution)/shard_map/all_gather | solution.py:54
  319.2 73.4 %copy-start = (f32[384,1024]{1,0:T(8,128)S(1)}, f32[384,1024]{1,0:T(8,128)}, u32[]{:S(2)}) copy-start(f32[384,1024]{1,0:T(8,128)} %reduce-scatter.2.cloned.1.call-done) | copy-start | bytes 4718596
Sparse Core Ops, SparseCore 0:
  252.3 65.1 reduce-scatter.1
  319.3 67.6 all-gather.1
where the time goes:
time: 401 us
  waiting for transfers between devices  340 us (85%)
  matrix products  15 us (4%)
  between operations  13.5 us (3%)
  starting transfers between devices  12.9 us (3%)
  local copies, waits for them, and re-layouts  11.5 us (3%)
  other arithmetic  7.65 us (2%)
    ppermute x3, waiting for transfers between devices, swapped(): lax.ppermute(value, axis, [(i, i ^ 1 << distance) for i in range(lax.axis...  207 us
    all_gather x1, waiting for transfers between devices, body(): gathered = lax.all_gather(summed, 'col', axis=0, tiled=True)  67.8 us
    reduce_scatter x1, waiting for transfers between devices, body(): summed = lax.psum_scatter(ladder, 'col', scatter_dimension=0, tiled=True)  65.3 us
    dot_general x4, matrix products, apply_tiles(): lax.dot_general(arrived, weights, contract, preferred_element_type=jnp.fl...  15 us
    ppermute x3, starting transfers between devices, swapped(): lax.ppermute(value, axis, [(i, i ^ 1 << distance) for i in range(lax.axis...  12.8 us
  transfers between devices with their start and end apart: 5, of which 5 were waited for; matrix products, arithmetic and copies ran while one was open for 4% of the time, Pallas kernels for 0%

commit v1 on v0

v1 whole, which is shorter than its diff:
```python
import functools

import jax
import jax.numpy as jnp
from jax import lax
from jax.experimental import pallas as pl
from jax.experimental.pallas import tpu as pltpu
from jax.sharding import PartitionSpec as P

MESH = pl.DeviceIdType.MESH
RING = 8
PIECES = 4
WINDOW = 4
FINAL_CUTS = 2
GROUP = 16


def kernel(
    amplitudes, integrals, allowed, partner, out,
    held, weights, own, to_core, from_core, to_x, from_x, ladder, mirror, finished,
    load_sem, ring_send, ring_recv, core_send, core_recv, x_send, x_recv, final_send, final_recv, local_sem,
):
    pieces, piece_rows, depth = amplitudes.shape
    half = pieces // 2
    arrivals = pieces * (RING - 1) // 2
    steps = half + arrivals
    block_rows = pieces * piece_rows
    quarter = integrals.shape[0] // 4
    out_rows = out.shape[0]

    blk, col = lax.axis_index("blk"), lax.axis_index("col")
    sector, member = blk // RING, blk % RING
    side, core = col // 2, col % 2
    first = sector * RING
    right = (first + (member + 1) % RING, col)
    left = (first + (member + RING - 1) % RING, col)
    core_peer = (blk, side * 2 + 1 - core)
    x_peer = (blk, (1 - side) * 2 + core)
    far_peer = (blk, (1 - side) * 2 + 1 - core)

    load_t = pltpu.make_async_copy(amplitudes, held.at[pl.ds(0, pieces)], load_sem.at[0])
    load_v = pltpu.make_async_copy(integrals, weights, load_sem.at[1])
    load_t.start()
    load_v.start()

    barrier = pltpu.get_barrier_semaphore()
    for peer in (right, left, core_peer, x_peer, far_peer):
        pl.semaphore_signal(barrier, inc=1, device_id=peer, device_id_type=MESH)
    pl.semaphore_wait(barrier, 5)

    def ring_copy(way, k, source=None):
        if source is None:
            start = k if way == 0 else (k + half) % pieces
            forward = pieces + 2 * (k - pieces) + way
            source = held.at[jnp.where(k < pieces, start, forward)]
        return pltpu.make_async_remote_copy(
            src_ref=source,
            dst_ref=held.at[pieces + 2 * k + way],
            send_sem=ring_send.at[way, k],
            recv_sem=ring_recv.at[way, k],
            device_id=(right, left)[way],
            device_id_type=MESH,
        )

    def core_copy(s):
        return pltpu.make_async_remote_copy(
            src_ref=to_core.at[s], dst_ref=from_core.at[s], send_sem=core_send.at[s], recv_sem=core_recv.at[s],
            device_id=core_peer, device_id_type=MESH,
        )

    def x_copy(s):
        return pltpu.make_async_remote_copy(
            src_ref=to_x.at[s], dst_ref=from_x.at[s], send_sem=x_send.at[s], recv_sem=x_recv.at[s],
            device_id=x_peer, device_id_type=MESH,
        )

    for k in range(WINDOW):
        ring_copy(0, k, amplitudes.at[k]).start()
        ring_copy(1, k, amplitudes.at[(k + half) % pieces]).start()

    load_v.wait()
    strip = 64
    width = depth // 2
    for tile in range(2):
        flag = allowed[sector, member, col * 2 + tile].astype(jnp.float32)
        factor = jnp.full((strip, width), flag, jnp.float32).astype(jnp.bfloat16)

        def mask(i, carry, tile=tile, factor=factor):
            at = (pl.ds(pl.multiple_of(i * strip, strip), strip), pl.ds(tile * width, width))
            weights[at] = weights[at] * factor
            return carry

        lax.fori_loop(0, integrals.shape[0] // strip, mask, 0)
    load_t.wait()

    def product(s, e_block):
        rows = held[pl.ds(2 * s, 2)].reshape(2 * piece_rows, depth)
        block = weights[pl.ds(pl.multiple_of(e_block * quarter, quarter), quarter), :]
        return lax.dot_general(rows, block, (((1,), (1,)), ((), ())), preferred_element_type=jnp.float32)

    def rows_at(s, way):
        t = s - half
        t_block = jnp.where(way == 0, member + RING - 1 - t // pieces, member + 1 + t // pieces) % RING
        t_piece = jnp.where(way == 0, t % pieces, (t % pieces + half) % pieces)
        block = jnp.where(s < half, member, t_block)
        piece = jnp.where(s < half, 2 * s + way, t_piece)
        return pl.multiple_of(block * block_rows + piece * piece_rows, piece_rows)

    def step(s, carry):
        @pl.when(jnp.logical_and(s >= half, s < steps))
        def _():
            t = s - half
            for way in range(2):
                ring_copy(way, t).wait_recv()

            @pl.when(t + WINDOW < arrivals)
            def _():
                for way in range(2):
                    ring_copy(way, t + WINDOW).start()

        @pl.when(s < steps)
        def _():
            to_core[s, 0] = product(s, (1 - core) * 2 + 1 - side)
            to_core[s, 1] = product(s, (1 - core) * 2 + side)
            core_copy(s).start()
            own[s, 0] = product(s, core * 2 + 1 - side)
            own[s, 1] = product(s, core * 2 + side)

        @pl.when(jnp.logical_and(s >= 1, s < steps + 1))
        def _():
            core_copy(s - 1).wait_recv()
            to_x[s - 1] = own[s - 1, 0] + from_core[s - 1, 0]
            x_copy(s - 1).start()

        @pl.when(s >= 2)
        def _():
            x_copy(s - 2).wait_recv()
            total = own[s - 2, 1] + from_core[s - 2, 1] + from_x[s - 2]
            ladder[pl.ds(rows_at(s - 2, 0), piece_rows), :] = total[:piece_rows]
            ladder[pl.ds(rows_at(s - 2, 1), piece_rows), :] = total[piece_rows:]

        return carry

    lax.fori_loop(0, steps + 2, step, 0)

    cut_rows = out_rows // FINAL_CUTS
    e_start = pl.multiple_of((core * 2 + side) * quarter, quarter)

    def final_copy(turn, cut, peer):
        return pltpu.make_async_remote_copy(
            src_ref=finished.at[turn, pl.ds(cut * cut_rows, cut_rows)],
            dst_ref=out.at[pl.ds(cut * cut_rows, cut_rows), pl.ds(e_start, quarter)],
            send_sem=final_send.at[turn, cut],
            recv_sem=final_recv.at[turn, cut],
            device_id=peer,
            device_id_type=MESH,
        )

    turns = (far_peer, x_peer, core_peer, None)
    for turn, peer in enumerate(turns):
        owner = col if peer is None else peer[1]
        for cut in range(FINAL_CUTS):
            start = owner * out_rows + cut * cut_rows

            def group(g, carry, turn=turn, cut=cut, start=start):
                at = pl.multiple_of(start + g * GROUP, GROUP)
                for i in range(GROUP):
                    mirror[pl.ds(at + i, 1), :] = ladder[pl.ds(partner[sector, at + i], 1), :]
                value = 0.5 * (ladder[pl.ds(at, GROUP), :] - mirror[pl.ds(at, GROUP), :])
                finished[turn, pl.ds(pl.multiple_of(cut * cut_rows + g * GROUP, GROUP), GROUP), :] = value.astype(out.dtype)
                return carry

            lax.fori_loop(0, cut_rows // GROUP, group, 0)
            if peer is not None:
                final_copy(turn, cut, peer).start()
    mine = pltpu.make_async_copy(finished.at[3], out.at[:, pl.ds(e_start, quarter)], local_sem)
    mine.start()

    for turn, peer in enumerate(turns[:3]):
        for cut in range(FINAL_CUTS):
            final_copy(turn, cut, peer).wait()
    mine.wait()

    def drain_ring(k, carry):
        for way in range(2):
            ring_copy(way, k).wait_send()
        return carry

    def drain_sums(s, carry):
        core_copy(s).wait_send()
        x_copy(s).wait_send()
        return carry

    lax.fori_loop(0, arrivals, drain_ring, 0)
    lax.fori_loop(0, steps, drain_sums, 0)


def body(amplitudes, integrals, allowed, partner):
    rows, depth = amplitudes.shape
    e_rows = integrals.shape[0]
    pieces, piece_rows, quarter = PIECES, rows // PIECES, e_rows // 4
    arrivals = pieces * (RING - 1) // 2
    steps = pieces // 2 + arrivals
    pairs = rows * RING
    out_rows = pairs // 4
    f32, bf16 = jnp.float32, jnp.bfloat16
    dma = pltpu.SemaphoreType.DMA
    anywhere = pl.BlockSpec(memory_space=pl.ANY)
    scalars = pl.BlockSpec(memory_space=pltpu.SMEM)
    return pl.pallas_call(
        kernel,
        out_shape=jax.ShapeDtypeStruct((out_rows, e_rows), bf16),
        in_specs=[anywhere, anywhere, scalars, scalars],
        out_specs=anywhere,
        scratch_shapes=[
            pltpu.VMEM((RING * pieces, piece_rows, depth), bf16),
            pltpu.VMEM((e_rows, depth), bf16),
            pltpu.VMEM((steps, 2, 2 * piece_rows, quarter), f32),
            pltpu.VMEM((steps, 2, 2 * piece_rows, quarter), f32),
            pltpu.VMEM((steps, 2, 2 * piece_rows, quarter), f32),
            pltpu.VMEM((steps, 2 * piece_rows, quarter), f32),
            pltpu.VMEM((steps, 2 * piece_rows, quarter), f32),
            pltpu.VMEM((pairs, quarter), f32),
            pltpu.VMEM((pairs, quarter), f32),
            pltpu.VMEM((4, out_rows, quarter), bf16),
            dma((2,)),
            dma((2, arrivals)),
            dma((2, arrivals)),
            dma((steps,)),
            dma((steps,)),
            dma((steps,)),
            dma((steps,)),
            dma((3, FINAL_CUTS)),
            dma((3, FINAL_CUTS)),
            dma(()),
        ],
        compiler_params=pltpu.CompilerParams(
            collective_id=0, has_side_effects=True, vmem_limit_bytes=48 * 1024 * 1024
        ),
        cost_estimate=pl.CostEstimate(
            flops=2 * pairs * e_rows * depth, bytes_accessed=2 * (e_rows * depth + rows * depth + out_rows * e_rows), transcendentals=0
        ),
        name="ladder_residual",
    )(amplitudes.reshape(pieces, piece_rows, depth), integrals, allowed, partner)


def solution(mesh):
    return jax.shard_map(
        body,
        mesh=mesh,
        in_specs=(P("blk", "col"), P("blk", "col"), P(), P()),
        out_specs=P("col", "blk"),
        check_vma=False,
    )
```

time: 401 us -> 94.8 us (0.24)
  waiting for transfers between devices: 340 us -> 0 us
  Pallas kernels: 0 us -> 88.1 us
  matrix products: 15 us -> 0 us
  between operations: 13.5 us -> 0.01 us
  starting transfers between devices: 12.9 us -> 0 us
  other arithmetic: 7.65 us -> 0 us
  local copies, waits for them, and re-layouts: 11.5 us -> 5.76 us
    ppermute x3 -> x0, waiting for transfers between devices: 207 us -> none  [swapped(): lax.ppermute(value, axis, [(i, i ^ 1 << distance) for i in range(lax.axis...]
    pallas_call x0 -> x1, Pallas kernels: none -> 88.1 us  [body(): pl.pallas_call(kernel, out_shape=jax.ShapeDtypeStruct((out_rows, e_rows),...]
    all_gather x1 -> x0, waiting for transfers between devices: 67.8 us -> none  [body(): gathered = lax.all_gather(summed, 'col', axis=0, tiled=True)]
    reduce_scatter x1 -> x0, waiting for transfers between devices: 65.3 us -> none  [body(): summed = lax.psum_scatter(ladder, 'col', scatter_dimension=0, tiled=True)]
    dot_general x4 -> x0, matrix products: 15 us -> none  [apply_tiles(): lax.dot_general(arrived, weights, contract, preferred_element_type=jnp.fl...]
    ppermute x3 -> x0, starting transfers between devices: 12.8 us -> none  [swapped(): lax.ppermute(value, axis, [(i, i ^ 1 << distance) for i in range(lax.axis...]
    select_n x3 -> x0, other arithmetic: 5.74 us -> none  [the longest x2 4.93 us: body(): jnp.where(lower_half, jnp.concatenate([collected, incoming], axis=0), jnp...]
    gather x1 -> x0, local copies, waits for them, and re-layouts: 5.56 us -> none  [body(): summed = 0.5 * (summed - jnp.take(gathered, my_partners, axis=0))]
  transfers between devices with their start and end apart: 5 -> 0, of which waited for: 5 -> 0; matrix products, arithmetic and copies ran while one was open for 4% -> 0% of each run, Pallas kernels for 0% -> 0%
where the time goes in v1:
time: 94.8 us; the launch traced here: 93.9 us
  Pallas kernels  88.1 us (93%)
  local copies, waits for them, and re-layouts  5.76 us (6%)
    pallas_call x1, Pallas kernels, body(): pl.pallas_call(kernel, out_shape=jax.ShapeDtypeStruct((out_rows, e_rows),...  88.1 us
    unnamed x9, local copies, waits for them, and re-layouts  5.76 us

profile of v1, /device:TPU:1, one launch (start us, length us, event | category | flops | bytes accessed | tf_op | source)
XLA Modules:
  0.0 93.9 jit_solution(15308939465582466696)
XLA Ops:
  0.0 0.0 copy-start
  0.0 2.2 %copy-done = bf16[1024,2048]{1,0:T(8,128)(2,1)S(1)} copy-done((bf16[1024,2048]{1,0:T(8,128)(2,1)S(1)}, bf16[1024,2048]{1,0:T(8,128)(2,1)}, u32[]{:S(2)}) %copy-start) | copy-done | bytes 4194328
  2.2 0.0 copy-start.1
  2.2 1.1 %copy-done.1 = bf16[192,2048]{1,0:T(8,128)(2,1)S(1)} copy-done((bf16[192,2048]{1,0:T(8,128)(2,1)S(1)}, bf16[192,2048]{1,0:T(8,128)(2,1)}, u32[]{:S(2)}) %copy-start.1) | copy-done | bytes 786456
  3.3 0.0 copy-start.2
  3.3 0.8 copy-done.2
  4.1 0.0 copy-start.3
  4.1 0.8 copy-done.3
  4.9 88.1 %ladder_residual.1 = bf16[384,1024]{1,0:T(8,128)(2,1)S(1)} custom-call(bf16[4,48,2048]{2,1,0:T(8,128)(2,1)S(1)} %bitcast.1, bf16[1024,2048]{1,0:T(8,128)(2,1)S(1)} %copy-done, s32[8,8,8]{2,1,0:T(8,128)S(1)} %copy-done.3, s32[8,1536]{1,0:T(8,128)S(1)} %copy-done.2), custom_call_target="tpu_custom_call" | custom-call | flops 6442450944 | bytes 5767168 | tf_op jit(solution)/shard_map/ladder_residual/pallas_call | solution.py:210
  93.0 0.9 copy.6
Async XLA Ops:
  0.0 2.2 %copy-start = (bf16[1024,2048]{1,0:T(8,128)(2,1)S(1)}, bf16[1024,2048]{1,0:T(8,128)(2,1)}, u32[]{:S(2)}) copy-start(bf16[1024,2048]{1,0:T(8,128)(2,1)} %integrals.1) | copy-start | bytes 12582916
  2.2 1.1 %copy-start.1 = (bf16[192,2048]{1,0:T(8,128)(2,1)S(1)}, bf16[192,2048]{1,0:T(8,128)(2,1)}, u32[]{:S(2)}) copy-start(bf16[192,2048]{1,0:T(8,128)(2,1)} %param.4) | copy-start | bytes 2359300
  3.3 0.8 copy-start.2
  4.1 0.8 copy-start.3

commit v2 on v1

v2 whole, which is shorter than its diff:
```python
import functools

import jax
import jax.numpy as jnp
from jax import lax
from jax.experimental import pallas as pl
from jax.experimental.pallas import tpu as pltpu
from jax.sharding import PartitionSpec as P

MESH = pl.DeviceIdType.MESH
RING = 8
PIECES = 4
WINDOW = 4
FINAL_CUTS = 4
GROUP = 16
LANES = 128
SUM_LAG, PASS_LAG, PICK_LAG = 1, 3, 4


def kernel(
    amplitudes, integrals, allowed_in, partner_in, out,
    allowed, partner, held, weights, own, to_core, from_core, to_x, from_x, ladder, mirror, results, partners, chosen, rounded,
    load_sem, ring_send, ring_recv, core_send, core_recv, x_send, x_recv, row_send, row_recv, out_sem,
):
    pieces, piece_rows, depth = amplitudes.shape
    half = pieces // 2
    arrivals = pieces * (RING - 1) // 2
    steps = half + arrivals
    block_rows = pieces * piece_rows
    quarter = integrals.shape[0] // 4
    out_rows = out.shape[0]

    blk, col = lax.axis_index("blk"), lax.axis_index("col")
    sector, member = blk // RING, blk % RING
    side, core = col // 2, col % 2
    first = sector * RING
    right = (first + (member + 1) % RING, col)
    left = (first + (member + RING - 1) % RING, col)
    core_peer = (blk, side * 2 + 1 - core)
    x_peer = (blk, (1 - side) * 2 + core)

    load_t = pltpu.make_async_copy(amplitudes, held.at[pl.ds(0, pieces)], load_sem.at[0])
    load_v = pltpu.make_async_copy(integrals, weights, load_sem.at[1])
    load_allowed = pltpu.make_async_copy(allowed_in, allowed, load_sem.at[2])
    load_partner = pltpu.make_async_copy(partner_in, partner, load_sem.at[3])
    load_t.start()
    load_v.start()
    load_allowed.start()
    load_partner.start()

    barrier = pltpu.get_barrier_semaphore()
    for peer in (right, left, core_peer, x_peer):
        pl.semaphore_signal(barrier, inc=1, device_id=peer, device_id_type=MESH)
    pl.semaphore_wait(barrier, 4)

    def ring_copy(way, k, source=None):
        if source is None:
            start = k if way == 0 else (k + half) % pieces
            forward = pieces + 2 * (k - pieces) + way
            source = held.at[jnp.where(k < pieces, start, forward)]
        return pltpu.make_async_remote_copy(
            src_ref=source,
            dst_ref=held.at[pieces + 2 * k + way],
            send_sem=ring_send.at[way, k],
            recv_sem=ring_recv.at[way, k],
            device_id=(right, left)[way],
            device_id_type=MESH,
        )

    def row_copy(kind, s):
        place = results.at[s, core * 2 + (1 - side if kind == 2 else side)]
        return pltpu.make_async_remote_copy(
            src_ref=place, dst_ref=place, send_sem=row_send.at[kind, s], recv_sem=row_recv.at[kind, s],
            device_id=x_peer if kind == 0 else core_peer, device_id_type=MESH,
        )

    def core_copy(s):
        return pltpu.make_async_remote_copy(
            src_ref=to_core.at[s], dst_ref=from_core.at[s], send_sem=core_send.at[s], recv_sem=core_recv.at[s],
            device_id=core_peer, device_id_type=MESH,
        )

    def x_copy(s):
        return pltpu.make_async_remote_copy(
            src_ref=to_x.at[s], dst_ref=from_x.at[s], send_sem=x_send.at[s], recv_sem=x_recv.at[s],
            device_id=x_peer, device_id_type=MESH,
        )

    for k in range(WINDOW):
        ring_copy(0, k, amplitudes.at[k]).start()
        ring_copy(1, k, amplitudes.at[(k + half) % pieces]).start()

    ladder[...] = jnp.zeros_like(ladder)
    load_partner.wait()

    def spread(g, carry):
        for i in range(GROUP):
            value = partner[sector, col * out_rows + g * GROUP + i]
            partners[pl.ds(g * GROUP + i, 1), :] = jnp.full((1, LANES), value, jnp.int32)
        return carry

    lax.fori_loop(0, out_rows // GROUP, spread, 0)
    load_allowed.wait()
    load_v.wait()
    strip = 64
    width = depth // 2
    for tile in range(2):
        flag = allowed[sector, member, col * 2 + tile].astype(jnp.float32)
        factor = jnp.full((strip, width), flag, jnp.float32).astype(jnp.bfloat16)

        def mask(i, carry, tile=tile, factor=factor):
            at = (pl.ds(pl.multiple_of(i * strip, strip), strip), pl.ds(tile * width, width))
            weights[at] = weights[at] * factor
            return carry

        lax.fori_loop(0, integrals.shape[0] // strip, mask, 0)
    load_t.wait()

    def product(s, e_block):
        rows = held[pl.ds(2 * s, 2)].reshape(2 * piece_rows, depth)
        block = weights[pl.ds(pl.multiple_of(e_block * quarter, quarter), quarter), :]
        return lax.dot_general(rows, block, (((1,), (1,)), ((), ())), preferred_element_type=jnp.float32)

    def rows_at(s, way):
        t = s - half
        t_block = jnp.where(way == 0, member + RING - 1 - t // pieces, member + 1 + t // pieces) % RING
        t_piece = jnp.where(way == 0, t % pieces, (t % pieces + half) % pieces)
        block = jnp.where(s < half, member, t_block)
        piece = jnp.where(s < half, 2 * s + way, t_piece)
        return pl.multiple_of(block * block_rows + piece * piece_rows, piece_rows)

    def in_chunk(rows, s):
        first_rows, second_rows = rows_at(s, 0), rows_at(s, 1)
        return jnp.logical_or(
            jnp.logical_and(rows >= first_rows, rows < first_rows + piece_rows),
            jnp.logical_and(rows >= second_rows, rows < second_rows + piece_rows),
        )

    def pick(s):
        shape = (out_rows, 2 * piece_rows)
        mine = col * out_rows + lax.broadcasted_iota(jnp.int32, shape, 0)
        other = partners[:, : 2 * piece_rows]
        lane = lax.broadcasted_iota(jnp.int32, shape, 1)
        at_lane = jnp.where(lane < piece_rows, rows_at(s, 0) + lane, rows_at(s, 1) + lane - piece_rows)
        mine_here = in_chunk(mine, s)
        wanted = jnp.where(mine_here, mine, other)
        sign = jnp.where(mine_here, 1.0, -1.0)
        choice = jnp.where(wanted == at_lane, sign, 0.0).astype(jnp.bfloat16)
        mine_wide = col * out_rows + lax.broadcasted_iota(jnp.int32, (out_rows, LANES), 0)
        hit = jnp.logical_or(in_chunk(mine_wide, s), in_chunk(partners[...], s))
        for e_block in range(4):
            fresh = jnp.dot(choice, results[s, e_block], preferred_element_type=jnp.float32)
            for lanes in range(0, quarter, LANES):
                at = slice(e_block * quarter + lanes, e_block * quarter + lanes + LANES)
                chosen[:, at] = jnp.where(hit, fresh[:, lanes : lanes + LANES], chosen[:, at])

    def drain_ring(k, carry):
        for way in range(2):
            ring_copy(way, k).wait_send()
        return carry

    def drain_sums(s, carry):
        core_copy(s).wait_send()
        x_copy(s).wait_send()
        return carry

    def drain_rows(s, carry):
        for kind in range(3):
            row_copy(kind, s).wait_send()
        return carry

    def step(s, carry):
        @pl.when(jnp.logical_and(s >= half, s < steps))
        def _():
            t = s - half
            for way in range(2):
                ring_copy(way, t).wait_recv()

            @pl.when(t + WINDOW < arrivals)
            def _():
                for way in range(2):
                    ring_copy(way, t + WINDOW).start()

        @pl.when(s < steps)
        def _():
            to_core[s, 0] = product(s, (1 - core) * 2 + 1 - side)
            to_core[s, 1] = product(s, (1 - core) * 2 + side)
            core_copy(s).start()
            own[s, 0] = product(s, core * 2 + 1 - side)
            own[s, 1] = product(s, core * 2 + side)

        @pl.when(jnp.logical_and(s >= PASS_LAG, s < steps + PASS_LAG))
        def _():
            row_copy(0, s - PASS_LAG).wait_recv()
            row_copy(2, s - PASS_LAG).start()

        @pl.when(s == steps + PICK_LAG - 1)
        def _():
            lax.fori_loop(0, steps - 1, drain_rows, 0)

        @pl.when(s >= PICK_LAG)
        def _():
            row_copy(1, s - PICK_LAG).wait_recv()
            row_copy(2, s - PICK_LAG).wait_recv()
            pick(s - PICK_LAG)

        @pl.when(s == steps + 1)
        def _():
            lax.fori_loop(0, steps, drain_sums, 0)

        @pl.when(s < steps)
        def _():
            core_copy(s).wait_recv()
            to_x[s] = own[s, 0] + from_core[s, 0]
            x_copy(s).start()

        @pl.when(s == steps)
        def _():
            lax.fori_loop(0, arrivals, drain_ring, 0)

        @pl.when(jnp.logical_and(s >= SUM_LAG, s < steps + SUM_LAG))
        def _():
            before = s - SUM_LAG
            x_copy(before).wait_recv()
            total = own[before, 1] + from_core[before, 1] + from_x[before]
            for way in range(2):
                ladder[pl.ds(rows_at(before, way), piece_rows), :] = total[way * piece_rows : (way + 1) * piece_rows]
            for i in range(2 * piece_rows):
                other = partner[sector, rows_at(before, i // piece_rows) + i % piece_rows]
                mirror[pl.ds(i, 1), :] = ladder[pl.ds(other, 1), :]
            results[before, core * 2 + side] = (0.5 * (total - mirror[...])).astype(jnp.bfloat16)
            row_copy(0, before).start()
            row_copy(1, before).start()

        return carry

    lax.fori_loop(0, steps + PICK_LAG, step, 0)

    cut_rows = out_rows // FINAL_CUTS
    cuts = [pl.ds(cut * cut_rows, cut_rows) for cut in range(FINAL_CUTS)]
    outgoing = [pltpu.make_async_copy(rounded.at[at], out.at[at], out_sem.at[cut]) for cut, at in enumerate(cuts)]
    for at, copy in zip(cuts, outgoing):
        rounded[at, :] = chosen[at, :].astype(jnp.bfloat16)
        copy.start()

    for kind in range(3):
        row_copy(kind, steps - 1).wait_send()
    for copy in outgoing:
        copy.wait()


def body(amplitudes, integrals, allowed, partner):
    rows, depth = amplitudes.shape
    e_rows = integrals.shape[0]
    pieces, piece_rows, quarter = PIECES, rows // PIECES, e_rows // 4
    arrivals = pieces * (RING - 1) // 2
    steps = pieces // 2 + arrivals
    pairs = rows * RING
    out_rows = pairs // 4
    f32, bf16 = jnp.float32, jnp.bfloat16
    dma = pltpu.SemaphoreType.DMA
    anywhere = pl.BlockSpec(memory_space=pl.ANY)
    return pl.pallas_call(
        kernel,
        out_shape=jax.ShapeDtypeStruct((out_rows, e_rows), bf16),
        in_specs=[anywhere] * 4,
        out_specs=anywhere,
        scratch_shapes=[
            pltpu.SMEM(allowed.shape, jnp.int32),
            pltpu.SMEM(partner.shape, jnp.int32),
            pltpu.VMEM((RING * pieces, piece_rows, depth), bf16),
            pltpu.VMEM((e_rows, depth), bf16),
            pltpu.VMEM((steps, 2, 2 * piece_rows, quarter), f32),
            pltpu.VMEM((steps, 2, 2 * piece_rows, quarter), f32),
            pltpu.VMEM((steps, 2, 2 * piece_rows, quarter), f32),
            pltpu.VMEM((steps, 2 * piece_rows, quarter), f32),
            pltpu.VMEM((steps, 2 * piece_rows, quarter), f32),
            pltpu.VMEM((pairs, quarter), f32),
            pltpu.VMEM((2 * piece_rows, quarter), f32),
            pltpu.VMEM((steps, 4, 2 * piece_rows, quarter), bf16),
            pltpu.VMEM((out_rows, LANES), jnp.int32),
            pltpu.VMEM((out_rows, e_rows), f32),
            pltpu.VMEM((out_rows, e_rows), bf16),
            dma((4,)),
            dma((2, arrivals)),
            dma((2, arrivals)),
            dma((steps,)),
            dma((steps,)),
            dma((steps,)),
            dma((steps,)),
            dma((3, steps)),
            dma((3, steps)),
            dma((FINAL_CUTS,)),
        ],
        compiler_params=pltpu.CompilerParams(
            collective_id=0, has_side_effects=True, vmem_limit_bytes=56 * 1024 * 1024
        ),
        cost_estimate=pl.CostEstimate(
            flops=2 * pairs * e_rows * depth, bytes_accessed=2 * (e_rows * depth + rows * depth + out_rows * e_rows), transcendentals=0
        ),
        name="ladder_residual",
    )(amplitudes.reshape(pieces, piece_rows, depth), integrals, allowed, partner)


def solution(mesh):
    return jax.shard_map(
        body,
        mesh=mesh,
        in_specs=(P("blk", "col"), P("blk", "col"), P(), P()),
        out_specs=P("col", "blk"),
        check_vma=False,
    )
```

time: 94.8 us -> 84.7 us (0.89)
  Pallas kernels: 88.1 us -> 82.5 us
  local copies, waits for them, and re-layouts: 5.76 us -> 2.06 us
    pallas_call x1, Pallas kernels: 88.1 us -> 82.5 us  [body(): pl.pallas_call(kernel, out_shape=jax.ShapeDtypeStruct((out_rows, e_rows),...]
    unnamed x9 -> x1, local copies, waits for them, and re-layouts: 5.76 us -> 2.06 us
where the time goes in v2:
time: 84.7 us; the launch traced here: 84.6 us
  Pallas kernels  82.5 us (97%)
  local copies, waits for them, and re-layouts  2.06 us (2%)
    pallas_call x1, Pallas kernels, body(): pl.pallas_call(kernel, out_shape=jax.ShapeDtypeStruct((out_rows, e_rows),...  82.5 us
    unnamed x1, local copies, waits for them, and re-layouts  2.06 us

profile of v2, /device:TPU:1, one launch (start us, length us, event | category | flops | bytes accessed | tf_op | source)
XLA Modules:
  0.0 84.6 jit_solution(5091455003714715852)
XLA Ops:
  0.0 82.5 %ladder_residual.1 = bf16[384,1024]{1,0:T(8,128)(2,1)} custom-call(bf16[4,48,2048]{2,1,0:T(8,128)(2,1)} %bitcast.1, bf16[1024,2048]{1,0:T(8,128)(2,1)} %integrals.1, s32[8,8,8]{2,1,0:T(8,128)} %allowed_in.1, s32[8,1536]{1,0:T(8,128)} %partner_in.1), custom_call_target="tpu_custom_call" | custom-call | flops 6442450944 | bytes 5767168 | tf_op jit(solution)/shard_map/ladder_residual/pallas_call | solution.py:263
  82.5 2.1 %copy.6 = bf16[384,1024]{1,0:T(8,128)(2,1)} copy(bf16[384,1024]{1,0:T(8,128)(2,1)} %ladder_residual.1) | data formatting | bytes 1572864

commit v3 on v2

--- a/solution.py
+++ b/solution.py
@@ -19,8 +19,8 @@
 
 def kernel(
     amplitudes, integrals, allowed_in, partner_in, out,
-    allowed, partner, held, weights, own, to_core, from_core, to_x, from_x, ladder, mirror, results, partners, chosen, rounded,
-    load_sem, ring_send, ring_recv, core_send, core_recv, x_send, x_recv, row_send, row_recv, out_sem,
+    allowed, partner, held, weights, own, to_core, from_core, to_x, from_x, ladder, mirror, results, partners, chosen,
+    load_sem, ring_send, ring_recv, core_send, core_recv, x_send, x_recv, row_send, row_recv,
 ):
     pieces, piece_rows, depth = amplitudes.shape
     half = pieces // 2
@@ -236,17 +236,16 @@
 
     lax.fori_loop(0, steps + PICK_LAG, step, 0)
 
-    cut_rows = out_rows // FINAL_CUTS
-    cuts = [pl.ds(cut * cut_rows, cut_rows) for cut in range(FINAL_CUTS)]
-    outgoing = [pltpu.make_async_copy(rounded.at[at], out.at[at], out_sem.at[cut]) for cut, at in enumerate(cuts)]
-    for at, copy in zip(cuts, outgoing):
-        rounded[at, :] = chosen[at, :].astype(jnp.bfloat16)
-        copy.start()
-
+    strip_rows = out_rows // FINAL_CUTS
+
+    def round_strip(i, carry):
+        at = pl.ds(pl.multiple_of(i * strip_rows, strip_rows), strip_rows)
+        out[at, :] = chosen[at, :].astype(jnp.bfloat16)
+        return carry
+
+    lax.fori_loop(0, FINAL_CUTS, round_strip, 0)
     for kind in range(3):
         row_copy(kind, steps - 1).wait_send()
-    for copy in outgoing:
-        copy.wait()
 
 
 def body(amplitudes, integrals, allowed, partner):
@@ -262,9 +261,9 @@
     anywhere = pl.BlockSpec(memory_space=pl.ANY)
     return pl.pallas_call(
         kernel,
-        out_shape=jax.ShapeDtypeStruct((out_rows, e_rows), bf16),
+        out_shape=pltpu.VMEM((out_rows, e_rows), bf16),
         in_specs=[anywhere] * 4,
-        out_specs=anywhere,
+        out_specs=pl.BlockSpec(memory_space=pltpu.VMEM),
         scratch_shapes=[
             pltpu.SMEM(allowed.shape, jnp.int32),
             pltpu.SMEM(partner.shape, jnp.int32),
@@ -280,7 +279,6 @@
             pltpu.VMEM((steps, 4, 2 * piece_rows, quarter), bf16),
             pltpu.VMEM((out_rows, LANES), jnp.int32),
             pltpu.VMEM((out_rows, e_rows), f32),
-            pltpu.VMEM((out_rows, e_rows), bf16),
             dma((4,)),
             dma((2, arrivals)),
             dma((2, arrivals)),
@@ -290,7 +288,6 @@
             dma((steps,)),
             dma((3, steps)),
             dma((3, steps)),
-            dma((FINAL_CUTS,)),
         ],
         compiler_params=pltpu.CompilerParams(
             collective_id=0, has_side_effects=True, vmem_limit_bytes=56 * 1024 * 1024

time: 84.7 us -> 82.7 us (0.976)
  local copies, waits for them, and re-layouts: 2.06 us -> 0.88 us
    unnamed x1, local copies, waits for them, and re-layouts: 2.06 us -> 0.88 us
where the time goes in v3:
time: 82.7 us; the launch traced here: 82.6 us
  Pallas kernels  81.7 us (99%)
  local copies, waits for them, and re-layouts  0.88 us (1%)
    pallas_call x1, Pallas kernels, body(): pl.pallas_call(kernel, out_shape=pltpu.VMEM((out_rows, e_rows), bf16), in...  81.7 us

profile of v3, /device:TPU:1, one launch (start us, length us, event | category | flops | bytes accessed | tf_op | source)
XLA Modules:
  0.0 82.6 jit_solution(5685356596368913955)
XLA Ops:
  0.0 81.7 %ladder_residual.1 = bf16[384,1024]{1,0:T(8,128)(2,1)S(1)} custom-call(bf16[4,48,2048]{2,1,0:T(8,128)(2,1)} %bitcast.1, bf16[1024,2048]{1,0:T(8,128)(2,1)} %integrals.1, s32[8,8,8]{2,1,0:T(8,128)} %allowed_in.1, s32[8,1536]{1,0:T(8,128)} %partner_in.1), custom_call_target="tpu_custom_call" | custom-call | flops 6442450944 | bytes 5767168 | tf_op jit(solution)/shard_map/ladder_residual/pallas_call | solution.py:262
  81.7 0.9 %copy.6 = bf16[384,1024]{1,0:T(8,128)(2,1)} copy(bf16[384,1024]{1,0:T(8,128)(2,1)S(1)} %ladder_residual.1) | data formatting | bytes 1572864

commit v4 on v3

--- a/solution.py
+++ b/solution.py
@@ -68,7 +68,7 @@
         )
 
     def row_copy(kind, s):
-        place = results.at[s, core * 2 + (1 - side if kind == 2 else side)]
+        place = results.at[s, core * 2 + side] if kind == 0 else results.at[s, pl.ds(core * 2, 2)]
         return pltpu.make_async_remote_copy(
             src_ref=place, dst_ref=place, send_sem=row_send.at[kind, s], recv_sem=row_recv.at[kind, s],
             device_id=x_peer if kind == 0 else core_peer, device_id_type=MESH,
@@ -165,7 +165,7 @@
         return carry
 
     def drain_rows(s, carry):
-        for kind in range(3):
+        for kind in range(2):
             row_copy(kind, s).wait_send()
         return carry
 
@@ -192,7 +192,7 @@
         @pl.when(jnp.logical_and(s >= PASS_LAG, s < steps + PASS_LAG))
         def _():
             row_copy(0, s - PASS_LAG).wait_recv()
-            row_copy(2, s - PASS_LAG).start()
+            row_copy(1, s - PASS_LAG).start()
 
         @pl.when(s == steps + PICK_LAG - 1)
         def _():
@@ -201,7 +201,6 @@
         @pl.when(s >= PICK_LAG)
         def _():
             row_copy(1, s - PICK_LAG).wait_recv()
-            row_copy(2, s - PICK_LAG).wait_recv()
             pick(s - PICK_LAG)
 
         @pl.when(s == steps + 1)
@@ -230,7 +229,6 @@
                 mirror[pl.ds(i, 1), :] = ladder[pl.ds(other, 1), :]
             results[before, core * 2 + side] = (0.5 * (total - mirror[...])).astype(jnp.bfloat16)
             row_copy(0, before).start()
-            row_copy(1, before).start()
 
         return carry
 
@@ -244,7 +242,7 @@
         return carry
 
     lax.fori_loop(0, FINAL_CUTS, round_strip, 0)
-    for kind in range(3):
+    for kind in range(2):
         row_copy(kind, steps - 1).wait_send()
 
 
@@ -286,8 +284,8 @@
             dma((steps,)),
             dma((steps,)),
             dma((steps,)),
-            dma((3, steps)),
-            dma((3, steps)),
+            dma((2, steps)),
+            dma((2, steps)),
         ],
         compiler_params=pltpu.CompilerParams(
             collective_id=0, has_side_effects=True, vmem_limit_bytes=56 * 1024 * 1024

time: 82.7 us -> 82.4 us (level)
  no operation moved by 1% of the time
where the time goes in v4:
time: 82.4 us
  Pallas kernels  81.5 us (99%)
  local copies, waits for them, and re-layouts  0.88 us (1%)
    pallas_call x1, Pallas kernels, body(): pl.pallas_call(kernel, out_shape=pltpu.VMEM((out_rows, e_rows), bf16), in...  81.5 us

profile of v4, /device:TPU:1, one launch (start us, length us, event | category | flops | bytes accessed | tf_op | source)
XLA Modules:
  0.0 82.4 jit_solution(9111164766474884986)
XLA Ops:
  0.0 81.5 %ladder_residual.1 = bf16[384,1024]{1,0:T(8,128)(2,1)S(1)} custom-call(bf16[4,48,2048]{2,1,0:T(8,128)(2,1)} %bitcast.1, bf16[1024,2048]{1,0:T(8,128)(2,1)} %integrals.1, s32[8,8,8]{2,1,0:T(8,128)} %allowed_in.1, s32[8,1536]{1,0:T(8,128)} %partner_in.1), custom_call_target="tpu_custom_call" | custom-call | flops 6442450944 | bytes 5767168 | tf_op jit(solution)/shard_map/ladder_residual/pallas_call | solution.py:260
  81.5 0.9 %copy.6 = bf16[384,1024]{1,0:T(8,128)(2,1)} copy(bf16[384,1024]{1,0:T(8,128)(2,1)S(1)} %ladder_residual.1) | data formatting | bytes 1572864
